TPU v7x, 32 devices: a whole 2x2x4 slice. The times are simulated.
32 devices in a mesh: seq: 16 (over z, y, core), head: 2 (over x).
Axes of the slice: x: 2, y: 2, z: 4, core: 2. Of those that a mesh axis runs over, the one named last changes fastest.
Arguments:
- queries: bfloat16 [1024, 2048], P('seq', 'head'), may hold values from -15 to 15
- cache_keys: bfloat16 [2, 16384, 128], P('head', 'seq'), may hold values from -6 to 6
- cache_values: bfloat16 [2, 16384, 128], P('head', 'seq'), may hold values from -6 to 6
- new_keys: bfloat16 [1024, 256], P('seq', 'head'), may hold values from -9.5625 to 9.5625
- new_values: bfloat16 [1024, 256], P('seq', 'head'), may hold values from -6 to 6
- cache_len: int32 [16], P('seq'), may hold values from 256 to 1024, as said below
- span_rank: int32 [1024], replicated, may hold values from 0 to 1023, each once
- out_weight: bfloat16 [2048, 8192], P('head', 'seq'), may hold values from -0.125 to 0.125
Outputs:
- projected: bfloat16 [1024, 8192], P('head', 'seq')
Inputs may be any that keep to these rules, and one draw needn't show every extreme that they name: `cache_len`: each shard holds at least 256 filled positions; one shard is full in every draw.
All inputs are finite; a program needn't handle non-finite values.
Results may differ from a plain program's by a relative error of at most 0.006.
Values may be sent and summed in bfloat16 or wider, within the bound.
A program may use at most 64 MiB of HBM per device.

v0:
```python
import functools
import math

import jax
import jax.numpy as jnp
from jax import lax
from jax.experimental import pallas as pl
from jax.experimental.pallas import tpu as pltpu
from jax.sharding import PartitionSpec as P

MESH = pl.DeviceIdType.MESH
HD = 128
AUG = 144
PART = 136
FILL = -1e30
SCALE = math.log2(math.e) / math.sqrt(HD)
F32 = jnp.float32
BF16 = jnp.bfloat16


def dot(a, b):
    return jnp.dot(a, b, preferred_element_type=F32)


def kernel(
    zs_count, heads, toks, qph,
    q_ref, k_ref, v_ref, nk_ref, nv_ref, len_ref, rank_ref, w_ref, out_ref,
    qall, k1, v1, nkv, k2, v2, nkv_y, krank, part, corebuf, zsend, zrecv, aall, facc, xs, xr,
    qz_s, qz_r, qc_s, qc_r, kv_s, kv_r, pc_s, pc_r, pz_s, pz_r,
    az_s, az_r, ay_s, ay_r, ac_s, ac_r, ad_s, ad_r, x_s, x_r,
):
    cache = k_ref.shape[0]
    rows = toks * qph
    fresh = 2 * toks
    me = lax.axis_index("seq")
    my_head = lax.axis_index("head")
    c = lax.rem(me, 2)
    y = lax.rem(me // 2, 2)
    z = me // 4
    core_peer = me + 1 - 2 * c
    y_peer = me + 2 - 4 * y

    def seq_id(other):
        return {"seq": other}

    def zdev(other):
        return other * 4 + y * 2 + c

    barrier = pltpu.get_barrier_semaphore()
    pl.semaphore_signal(barrier, inc=1, device_id=seq_id(core_peer), device_id_type=MESH)
    pl.semaphore_signal(barrier, inc=1, device_id=seq_id(y_peer), device_id_type=MESH)
    for d in range(1, zs_count):
        pl.semaphore_signal(
            barrier, inc=1, device_id=seq_id(zdev(lax.rem(z + d, zs_count))), device_id_type=MESH
        )
    for e in range(1, heads):
        pl.semaphore_signal(
            barrier, inc=1, device_id={"head": lax.rem(my_head + e, heads)}, device_id_type=MESH
        )

    q_rows = jnp.concatenate([q_ref[:, h * HD:(h + 1) * HD] for h in range(qph)], axis=0)
    qall[z * 2 + c] = q_rows.astype(F32).T.astype(BF16)
    pl.semaphore_wait(barrier, zs_count + heads)

    def remote(src, dst, send, recv, device):
        return pltpu.make_async_remote_copy(
            src_ref=src, dst_ref=dst, send_sem=send, recv_sem=recv,
            device_id=device, device_id_type=MESH,
        )

    def q_to_z(d):
        slot = z * 2 + c
        return remote(
            qall.at[slot], qall.at[slot], qz_s.at[d], qz_r.at[d],
            seq_id(zdev(lax.rem(z + d, zs_count))),
        )

    def q_to_core(d):
        slot = lax.rem(z - d + zs_count, zs_count) * 2 + c
        return remote(qall.at[slot], qall.at[slot], qc_s.at[d], qc_r.at[d], seq_id(core_peer))

    q_to_core(0).start()
    for d in range(1, zs_count):
        q_to_z(d).start()

    length = len_ref[0]
    used = lax.broadcasted_iota(jnp.int32, (cache, HD), 0) < length
    k1[...] = jnp.where(used, k_ref[...].astype(F32), k_ref[0:1, :].astype(F32)).astype(BF16)
    nkv[0:toks] = nk_ref[...]
    nkv[toks:fresh] = nv_ref[...]
    k_to_y = remote(k1, k2.at[pl.ds(0, cache)], kv_s.at[0], kv_r.at[0], seq_id(y_peer))
    n_to_y = remote(nkv, nkv_y, kv_s.at[1], kv_r.at[1], seq_id(y_peer))
    v_to_y = remote(v1, v2.at[:, pl.ds(0, cache)], kv_s.at[2], kv_r.at[2], seq_id(y_peer))
    n_to_y.start()
    k_to_y.start()
    v1[0:HD] = jnp.where(used, v_ref[...].astype(F32), 0.0).T.astype(BF16)
    used_lane = lax.broadcasted_iota(jnp.int32, (AUG - HD, cache), 1) < length
    v1[HD:AUG] = jnp.where(used_lane, 1.0, 0.0).astype(BF16)
    v_to_y.start()

    lane = lax.broadcasted_iota(jnp.int32, (1, HD), 1)

    def chip_ranks(chip, half):
        row = rank_ref[pl.ds(chip, 1), :]
        turned = pltpu.roll(row, toks, 1)
        first = jnp.where(lane < toks, row, turned)
        second = jnp.where(lane < toks, turned, row)
        return jnp.where(half == 0, first, second).astype(F32)

    own_chip = z * 2 + y
    both = jnp.where(lane < toks, chip_ranks(own_chip, c), chip_ranks(z * 2 + 1 - y, c))
    krank[...] = jnp.broadcast_to(both, (HD, HD)).T

    half_rows = rows // 2

    def first_pass(slot):
        for half in range(2):
            cols = slice(half * half_rows, (half + 1) * half_rows)
            s = dot(k1[...], qall[slot, :, cols])
            top = jnp.max(s, axis=0, keepdims=True)
            weights = jnp.exp2((s - top) * SCALE).astype(BF16)
            summed = dot(v1[...], weights)
            part[slot, 0:HD, cols] = summed[0:HD]
            stat = lax.broadcasted_iota(jnp.int32, (8, half_rows), 0)
            part[slot, HD:PART, cols] = jnp.where(stat == 0, summed[HD:HD + 1], top)

    def second_pass(slot, zz, half_of):
        q_rank = chip_ranks(zz * 2 + y, half_of)
        q_rank = jnp.concatenate([q_rank] * (half_rows // HD), axis=1)
        k_rank = jnp.concatenate([krank[...]] * (half_rows // HD), axis=1)
        usable = k_rank <= q_rank
        for half in range(2):
            cols = slice(half * half_rows, (half + 1) * half_rows)
            qt = qall[slot, :, cols]
            s = dot(k2[0:cache], qt)
            s_new = jnp.where(usable, dot(k2[cache:cache + fresh], qt), FILL)
            top_1 = part[slot, HD + 1:HD + 2, cols]
            sum_1 = part[slot, HD:HD + 1, cols]
            top = jnp.maximum(jnp.max(s, axis=0, keepdims=True), top_1)
            top = jnp.maximum(top, jnp.max(s_new, axis=0, keepdims=True))
            weights = jnp.exp2((s - top) * SCALE).astype(BF16)
            weights_new = jnp.exp2((s_new - top) * SCALE).astype(BF16)
            summed = dot(v2[:, 0:cache], weights) + dot(v2[:, cache:cache + fresh], weights_new)
            keep = jnp.exp2((top_1 - top) * SCALE)
            part[slot, 0:HD, cols] = part[slot, 0:HD, cols] * keep + summed[0:HD]
            total = sum_1 * keep + summed[HD:HD + 1]
            stat = lax.broadcasted_iota(jnp.int32, (8, half_rows), 0)
            part[slot, HD:PART, cols] = jnp.where(stat == 0, total, top)

    def pass_one(d, carry):
        zz = lax.rem(z - d + zs_count, zs_count)

        @pl.when(d > 0)
        def _():
            q_to_z(d).wait_recv()
            q_to_core(d).start()

        first_pass(zz * 2 + c)
        q_to_core(d).wait_recv()
        first_pass(zz * 2 + 1 - c)
        return carry

    lax.fori_loop(0, zs_count, pass_one, 0)

    n_to_y.wait_recv()
    k_to_y.wait_recv()
    k2[cache:cache + toks] = nkv[0:toks]
    k2[cache + toks:cache + fresh] = nkv_y[0:toks]
    new_values = jnp.concatenate([nkv[toks:fresh], nkv_y[toks:fresh]], axis=0)
    v_to_y.wait_recv()
    v2[0:HD, cache:cache + fresh] = new_values.astype(F32).T.astype(BF16)
    v2[HD:AUG, cache:cache + fresh] = jnp.ones((AUG - HD, fresh), BF16)

    def p_to_core(d):
        zz = lax.rem(z - d + zs_count, zs_count)
        at = d - 1
        return remote(
            part.at[zz * 2 + 1 - c], corebuf.at[at], pc_s.at[at], pc_r.at[at], seq_id(core_peer)
        )

    def p_to_z(d):
        zz = lax.rem(z - d + zs_count, zs_count)
        return remote(zsend.at[d], zrecv.at[d], pz_s.at[d], pz_r.at[d], seq_id(zdev(zz)))

    def merged(slot, at):
        sum_a, top_a = part[slot, HD:HD + 1, :], part[slot, HD + 1:HD + 2, :]
        sum_b, top_b = corebuf[at, HD:HD + 1, :], corebuf[at, HD + 1:HD + 2, :]
        top = jnp.maximum(top_a, top_b)
        fac_a = jnp.exp2((top_a - top) * SCALE)
        fac_b = jnp.exp2((top_b - top) * SCALE)
        total = sum_a * fac_a + sum_b * fac_b
        level = top * SCALE + jnp.log2(total)
        inverse = 1.0 / total
        mean = part[slot, 0:HD, :] * (fac_a * inverse) + corebuf[at, 0:HD, :] * (fac_b * inverse)
        return mean, level

    def pass_two(d, carry):
        zz = lax.rem(z - d + zs_count, zs_count)
        second_pass(zz * 2 + 1 - c, zz, 1 - c)
        p_to_core(d).start()
        second_pass(zz * 2 + c, zz, c)
        p_to_core(d).wait_recv()

        @pl.when(d < zs_count)
        def _():
            mean, level = merged(zz * 2 + c, d - 1)
            zsend[d, 0:HD] = mean.astype(BF16)
            high = level.astype(BF16).astype(F32)
            middle = (level - high).astype(BF16).astype(F32)
            low = level - high - middle
            stat = lax.broadcasted_iota(jnp.int32, (AUG - HD, rows), 0)
            terms = jnp.where(stat == 0, high, jnp.where(stat == 1, middle, low))
            zsend[d, HD:AUG] = terms.astype(BF16)
            p_to_z(d).start()

        return carry

    lax.fori_loop(1, zs_count + 1, pass_two, 0)

    means, levels = [], []
    mean, level = merged(z * 2 + c, zs_count - 1)
    means.append(mean)
    levels.append(level)
    for d in range(1, zs_count):
        p_to_z(d).wait_recv()
        terms = zrecv[d, HD:AUG].astype(F32)
        levels.append(terms[0:1] + terms[1:2] + terms[2:3])
        means.append(zrecv[d, 0:HD].astype(F32))
    top = functools.reduce(jnp.maximum, levels)
    factors = [jnp.exp2(level - top) for level in levels]
    inverse = 1.0 / sum(factors)
    attended = sum(mean * (factor * inverse) for mean, factor in zip(means, factors))
    attended = attended.T.astype(BF16)
    own = pl.ds(pl.multiple_of(me * toks, toks), toks)
    for h in range(qph):
        aall[own, h * HD:(h + 1) * HD] = attended[h * toks:(h + 1) * toks]

    chip_rows = 4 * toks
    per_head = zs_count // heads

    def spot(zz, yy, cc):
        return pl.ds(pl.multiple_of((zz * 4 + yy * 2 + cc) * toks, toks), toks)

    def a_move(s, step):
        where = spot(s, y, c)
        side = 0 if step > 0 else 1
        return remote(
            aall.at[where], aall.at[where], az_s.at[side, s], az_r.at[s], seq_id(zdev(z + step))
        )

    def a_to_y(s):
        where = spot(s, y, c)
        return remote(aall.at[where], aall.at[where], ay_s.at[s], ay_r.at[s], seq_id(y_peer))

    def a_to_core(s):
        where = spot(s, y, c)
        return remote(aall.at[where], aall.at[where], ac_s.at[s], ac_r.at[s], seq_id(core_peer))

    def ay_to_core(s):
        where = spot(s, 1 - y, c)
        return remote(aall.at[where], aall.at[where], ad_s.at[s], ad_r.at[s], seq_id(core_peer))

    def x_send(s):
        owner = s // per_head
        slot = lax.rem(my_head - owner + heads, heads) * per_head + lax.rem(s, per_head)
        return remote(xs.at[s], xr.at[slot], x_s.at[s], x_r.at[slot], {"head": owner})

    def product(s):
        lines = pl.ds(pl.multiple_of(s * chip_rows, chip_rows), chip_rows)
        return dot(aall[lines, :], w_ref[...])

    @pl.when(z < zs_count - 1)
    def _():
        a_move(z, 1).start()

    @pl.when(z > 0)
    def _():
        a_move(z, -1).start()

    a_to_y(z).start()
    a_to_core(z).start()

    def spread(i, carry):
        for step in (1, -1):
            s = z - step * i
            here = jnp.logical_and(s >= 0, s < zs_count)

            @pl.when(jnp.logical_and(here, i < zs_count))
            def _():
                a_move(s, step).wait_recv()
                onward = z < zs_count - 1 if step > 0 else z > 0

                @pl.when(onward)
                def _():
                    a_move(s, step).start()

                a_to_y(s).start()
                a_to_core(s).start()

        for step in (1, -1):
            s = z - step * (i - 1)
            here = jnp.logical_and(s >= 0, s < zs_count)
            if step < 0:
                here = jnp.logical_and(here, i > 1)

            @pl.when(here)
            def _():
                a_to_y(s).wait_recv()
                ay_to_core(s).start()

        for step in (1, -1):
            s = z - step * (i - 2)
            here = jnp.logical_and(jnp.logical_and(s >= 0, s < zs_count), i >= 2)
            if step < 0:
                here = jnp.logical_and(here, i > 2)

            @pl.when(jnp.logical_and(here, s // per_head != my_head))
            def _():
                a_to_core(s).wait_recv()
                ay_to_core(s).wait_recv()
                xs[s] = product(s).astype(BF16)
                x_send(s).start()

        return carry

    lax.fori_loop(1, zs_count + 2, spread, 0)

    for k in range(per_head):
        s = my_head * per_head + k
        a_to_core(s).wait_recv()
        ay_to_core(s).wait_recv()
        facc[k] = product(s)

    for k in range(per_head):
        total = facc[k]
        for e in range(1, heads):
            slot = e * per_head + k
            remote(
                xs.at[0], xr.at[slot], x_s.at[0], x_r.at[slot],
                {"head": lax.rem(my_head + e, heads)},
            ).wait_recv()
            total = total + xr[slot].astype(F32)
        out_ref[k * chip_rows:(k + 1) * chip_rows] = total.astype(BF16)

    n_to_y.wait_send()
    k_to_y.wait_send()
    v_to_y.wait_send()

    def finish(d, carry):
        q_to_core(d).wait_send()
        p_to_core(d + 1).wait_send()
        a_to_y(d).wait_send()
        a_to_core(d).wait_send()
        ay_to_core(d).wait_send()

        @pl.when(d > 0)
        def _():
            q_to_z(d).wait_send()
            p_to_z(d).wait_send()

        @pl.when(jnp.logical_and(z < zs_count - 1, d <= z))
        def _():
            a_move(d, 1).wait_send()

        @pl.when(jnp.logical_and(z > 0, d >= z))
        def _():
            a_move(d, -1).wait_send()

        @pl.when(d // per_head != my_head)
        def _():
            x_send(d).wait_send()

        return carry

    lax.fori_loop(0, zs_count, finish, 0)


def body(queries, cache_keys, cache_values, new_keys, new_values, cache_len, span_rank, out_weight):
    toks = queries.shape[0]
    qph = queries.shape[1] // HD
    cache = cache_keys.shape[1]
    rows = toks * qph
    width = out_weight.shape[1]
    shards = lax.axis_size("seq")
    heads = lax.axis_size("head")
    zs = shards // 4
    span = span_rank.shape[0]
    out_rows = span // heads
    vmem = pl.BlockSpec(memory_space=pltpu.VMEM)
    smem = pl.BlockSpec(memory_space=pltpu.SMEM)
    sems = [(zs,)] * 4 + [(3,)] * 2 + [(zs,)] * 4 + [(2, zs)] + [(zs,)] * 9
    per_head = zs // heads
    return pl.pallas_call(
        functools.partial(kernel, zs, heads, toks, qph),
        out_shape=jax.ShapeDtypeStruct((out_rows, width), BF16),
        in_specs=[vmem] * 5 + [smem] + [vmem] * 2,
        out_specs=vmem,
        scratch_shapes=[
            pltpu.VMEM((zs * 2, HD, rows), BF16),
            pltpu.VMEM((cache, HD), BF16),
            pltpu.VMEM((AUG, cache), BF16),
            pltpu.VMEM((2 * toks, HD), BF16),
            pltpu.VMEM((cache + 2 * toks, HD), BF16),
            pltpu.VMEM((AUG, cache + 2 * toks), BF16),
            pltpu.VMEM((2 * toks, HD), BF16),
            pltpu.VMEM((HD, HD), F32),
            pltpu.VMEM((zs * 2, PART, rows), F32),
            pltpu.VMEM((zs, PART, rows), F32),
            pltpu.VMEM((zs, AUG, rows), BF16),
            pltpu.VMEM((zs, AUG, rows), BF16),
            pltpu.VMEM((span, qph * HD), BF16),
            pltpu.VMEM((per_head, 4 * toks, width), F32),
            pltpu.VMEM((zs, 4 * toks, width), BF16),
            pltpu.VMEM((zs, 4 * toks, width), BF16),
        ] + [pltpu.SemaphoreType.DMA(count) for count in sems],
        compiler_params=pltpu.CompilerParams(
            collective_id=0, has_side_effects=True, vmem_limit_bytes=56 * 1024 * 1024
        ),
    )(
        queries, cache_keys[0], cache_values[0], new_keys, new_values, cache_len,
        span_rank.reshape(span // HD, HD), out_weight,
    )


def solution(mesh):
    return jax.shard_map(
        body,
        mesh=mesh,
        in_specs=(
            P("seq", "head"),
            P("head", "seq", None),
            P("head", "seq", None),
            P("seq", "head"),
            P("seq", "head"),
            P("seq"),
            P(),
            P("head", "seq"),
        ),
        out_specs=P("head", "seq"),
        check_vma=False,
    )
```

profile of v0, /device:TPU:0, one launch (start us, length us, event | category | flops | bytes accessed | tf_op | source)
XLA Modules:
  0.0 77.6 jit_solution(13418926620374179304)
XLA Ops:
  0.7 75.1 %shard_map.82 = bf16[512,512]{1,0:T(8,128)(2,1)} custom-call(bf16[64,1024]{1,0:T(8,128)(2,1)} %q_ref.1, bf16[1024,128]{1,0:T(8,128)(2,1)} %bitcast.3, bf16[1024,128]{1,0:T(8,128)(2,1)} %bitcast.4, bf16[64,128]{1,0:T(8,128)(2,1)} %nk_ref.1, bf16[64,128]{1,0:T(8,128)(2,1)} %nv_ref.1, s32[1]{0:T(128)S(6)} %copy.10.len_ref, s32[8,128]{1,0:T(8,128)} %bitcast.5, ...), custom_call_target="tpu_custom_call" | custom-call | tf_op jit(solution)/shard_map/pallas_call | solution.py:393
  75.7 1.9 %copy.11 = bf16[512,512]{1,0:T(8,128)(2,1)} copy(bf16[512,512]{1,0:T(8,128)(2,1)} %shard_map.82) | data formatting | bytes 1048576
where the time goes:
time: 77.8 us; the launch traced here: 77.6 us
  Pallas kernels  75.1 us (97%)
  local copies, waits for them, and re-layouts  1.87 us (2%)
    pallas_call x1, Pallas kernels, body(): pl.pallas_call(functools.partial(kernel, zs, heads, toks, qph), out_shape...  75.1 us
    unnamed x1, local copies, waits for them, and re-layouts  1.87 us

commit v1 on v0

--- a/solution.py
+++ b/solution.py
@@ -26,12 +26,15 @@
     zs_count, heads, toks, qph,
     q_ref, k_ref, v_ref, nk_ref, nv_ref, len_ref, rank_ref, w_ref, out_ref,
     qall, k1, v1, nkv, k2, v2, nkv_y, krank, part, corebuf, zsend, zrecv, aall, facc, xs, xr,
+    s0, s1, s2, s3, p0, p1, p2, p3,
     qz_s, qz_r, qc_s, qc_r, kv_s, kv_r, pc_s, pc_r, pz_s, pz_r,
     az_s, az_r, ay_s, ay_r, ac_s, ac_r, ad_s, ad_r, x_s, x_r,
 ):
     cache = k_ref.shape[0]
     rows = toks * qph
     fresh = 2 * toks
+    s_buf = (s0, s1, s2, s3)
+    p_buf = (p0, p1, p2, p3)
     me = lax.axis_index("seq")
     my_head = lax.axis_index("head")
     c = lax.rem(me, 2)
@@ -68,20 +71,36 @@
             device_id=device, device_id_type=MESH,
         )
 
-    def q_to_z(d):
-        slot = z * 2 + c
+    def nearest(j):
+        short = jnp.minimum(z, zs_count - 1 - z)
+        paired = j <= 2 * short
+        away = jnp.where(paired, (j + 1) // 2, j - short)
+        up = jnp.where(paired, j % 2 == 0, z == short)
+        return z + jnp.where(up, away, -away)
+
+    def q_move(s, step):
+        slot = s * 2 + c
+        side = (1 - step) // 2
         return remote(
-            qall.at[slot], qall.at[slot], qz_s.at[d], qz_r.at[d],
-            seq_id(zdev(lax.rem(z + d, zs_count))),
+            qall.at[slot], qall.at[slot], qz_s.at[side, s], qz_r.at[s], seq_id(zdev(z + step))
         )
 
-    def q_to_core(d):
-        slot = lax.rem(z - d + zs_count, zs_count) * 2 + c
-        return remote(qall.at[slot], qall.at[slot], qc_s.at[d], qc_r.at[d], seq_id(core_peer))
-
-    q_to_core(0).start()
-    for d in range(1, zs_count):
-        q_to_z(d).start()
+    def q_to_core(s):
+        slot = s * 2 + c
+        return remote(qall.at[slot], qall.at[slot], qc_s.at[s], qc_r.at[s], seq_id(core_peer))
+
+    can_rise = z < zs_count - 1
+    can_fall = z > 0
+
+    @pl.when(can_rise)
+    def _():
+        q_move(z, 1).start()
+
+    @pl.when(can_fall)
+    def _():
+        q_move(z, -1).start()
+
+    q_to_core(z).start()
 
     length = len_ref[0]
     used = lax.broadcasted_iota(jnp.int32, (cache, HD), 0) < length
@@ -112,52 +131,92 @@
     krank[...] = jnp.broadcast_to(both, (HD, HD)).T
 
     half_rows = rows // 2
-
-    def first_pass(slot):
-        for half in range(2):
-            cols = slice(half * half_rows, (half + 1) * half_rows)
-            s = dot(k1[...], qall[slot, :, cols])
-            top = jnp.max(s, axis=0, keepdims=True)
-            weights = jnp.exp2((s - top) * SCALE).astype(BF16)
-            summed = dot(v1[...], weights)
+    parts = (slice(0, half_rows), slice(half_rows, rows))
+    stat = lax.broadcasted_iota(jnp.int32, (8, half_rows), 0)
+
+    def staged(count, score, weigh, gather):
+        for i in range(count + 2):
+            if i < count:
+                score(i)
+            if 1 <= i <= count:
+                weigh(i - 1)
+            if i >= 2:
+                gather(i - 2)
+
+    def first_pass(slots):
+        tiles = [(slot, cols) for slot in slots for cols in parts]
+        tops = {}
+
+        def score(i):
+            slot, cols = tiles[i]
+            s_buf[i][0:cache] = dot(k1[...], qall[slot, :, cols])
+
+        def weigh(i):
+            s = s_buf[i][0:cache]
+            tops[i] = jnp.max(s, axis=0, keepdims=True)
+            p_buf[i][0:cache] = jnp.exp2((s - tops[i]) * SCALE).astype(BF16)
+
+        def gather(i):
+            slot, cols = tiles[i]
+            summed = dot(v1[...], p_buf[i][0:cache])
             part[slot, 0:HD, cols] = summed[0:HD]
-            stat = lax.broadcasted_iota(jnp.int32, (8, half_rows), 0)
-            part[slot, HD:PART, cols] = jnp.where(stat == 0, summed[HD:HD + 1], top)
-
-    def second_pass(slot, zz, half_of):
-        q_rank = chip_ranks(zz * 2 + y, half_of)
-        q_rank = jnp.concatenate([q_rank] * (half_rows // HD), axis=1)
+            part[slot, HD:PART, cols] = jnp.where(stat == 0, summed[HD:HD + 1], tops[i])
+
+        staged(len(tiles), score, weigh, gather)
+
+    def second_pass(zz):
         k_rank = jnp.concatenate([krank[...]] * (half_rows // HD), axis=1)
-        usable = k_rank <= q_rank
-        for half in range(2):
-            cols = slice(half * half_rows, (half + 1) * half_rows)
-            qt = qall[slot, :, cols]
-            s = dot(k2[0:cache], qt)
-            s_new = jnp.where(usable, dot(k2[cache:cache + fresh], qt), FILL)
-            top_1 = part[slot, HD + 1:HD + 2, cols]
-            sum_1 = part[slot, HD:HD + 1, cols]
-            top = jnp.maximum(jnp.max(s, axis=0, keepdims=True), top_1)
+        tiles, usable = [], []
+        for half_of in (1 - c, c):
+            q_rank = chip_ranks(zz * 2 + y, half_of)
+            q_rank = jnp.concatenate([q_rank] * (half_rows // HD), axis=1)
+            for cols in parts:
+                tiles.append((zz * 2 + half_of, cols))
+                usable.append(q_rank)
+        old = [
+            (part[slot, HD:HD + 1, cols], part[slot, HD + 1:HD + 2, cols]) for slot, cols in tiles
+        ]
+        tops = {}
+
+        def score(i):
+            slot, cols = tiles[i]
+            s_buf[i][...] = dot(k2[...], qall[slot, :, cols])
+
+        def weigh(i):
+            s = s_buf[i][0:cache]
+            s_new = jnp.where(k_rank <= usable[i], s_buf[i][cache:cache + fresh], FILL)
+            top = jnp.maximum(jnp.max(s, axis=0, keepdims=True), old[i][1])
             top = jnp.maximum(top, jnp.max(s_new, axis=0, keepdims=True))
-            weights = jnp.exp2((s - top) * SCALE).astype(BF16)
-            weights_new = jnp.exp2((s_new - top) * SCALE).astype(BF16)
-            summed = dot(v2[:, 0:cache], weights) + dot(v2[:, cache:cache + fresh], weights_new)
-            keep = jnp.exp2((top_1 - top) * SCALE)
+            p_buf[i][0:cache] = jnp.exp2((s - top) * SCALE).astype(BF16)
+            p_buf[i][cache:cache + fresh] = jnp.exp2((s_new - top) * SCALE).astype(BF16)
+            tops[i] = top
+
+        def gather(i):
+            slot, cols = tiles[i]
+            summed = dot(v2[...], p_buf[i][...])
+            keep = jnp.exp2((old[i][1] - tops[i]) * SCALE)
             part[slot, 0:HD, cols] = part[slot, 0:HD, cols] * keep + summed[0:HD]
-            total = sum_1 * keep + summed[HD:HD + 1]
-            stat = lax.broadcasted_iota(jnp.int32, (8, half_rows), 0)
-            part[slot, HD:PART, cols] = jnp.where(stat == 0, total, top)
-
-    def pass_one(d, carry):
-        zz = lax.rem(z - d + zs_count, zs_count)
-
-        @pl.when(d > 0)
-        def _():
-            q_to_z(d).wait_recv()
-            q_to_core(d).start()
-
-        first_pass(zz * 2 + c)
-        q_to_core(d).wait_recv()
-        first_pass(zz * 2 + 1 - c)
+            total = old[i][0] * keep + summed[HD:HD + 1]
+            part[slot, HD:PART, cols] = jnp.where(stat == 0, total, tops[i])
+
+        staged(len(tiles), score, weigh, gather)
+
+    def pass_one(j, carry):
+        s = nearest(j)
+        step = jnp.where(s < z, 1, -1)
+
+        @pl.when(j > 0)
+        def _():
+            q_move(s, step).wait_recv()
+
+            @pl.when(jnp.where(s < z, z < zs_count - 1, z > 0))
+            def _():
+                q_move(s, step).start()
+
+            q_to_core(s).start()
+
+        q_to_core(s).wait_recv()
+        first_pass([s * 2 + c, s * 2 + 1 - c])
         return carry
 
     lax.fori_loop(0, zs_count, pass_one, 0)
@@ -195,27 +254,32 @@
         return mean, level
 
     def pass_two(d, carry):
-        zz = lax.rem(z - d + zs_count, zs_count)
-        second_pass(zz * 2 + 1 - c, zz, 1 - c)
-        p_to_core(d).start()
-        second_pass(zz * 2 + c, zz, c)
-        p_to_core(d).wait_recv()
-
-        @pl.when(d < zs_count)
-        def _():
-            mean, level = merged(zz * 2 + c, d - 1)
-            zsend[d, 0:HD] = mean.astype(BF16)
-            high = level.astype(BF16).astype(F32)
-            middle = (level - high).astype(BF16).astype(F32)
-            low = level - high - middle
-            stat = lax.broadcasted_iota(jnp.int32, (AUG - HD, rows), 0)
-            terms = jnp.where(stat == 0, high, jnp.where(stat == 1, middle, low))
-            zsend[d, HD:AUG] = terms.astype(BF16)
-            p_to_z(d).start()
+        @pl.when(d <= zs_count)
+        def _():
+            second_pass(lax.rem(z - d + zs_count, zs_count))
+            p_to_core(d).start()
+
+        @pl.when(d > 1)
+        def _():
+            at = d - 1
+            zz = lax.rem(z - at + zs_count, zs_count)
+            p_to_core(at).wait_recv()
+
+            @pl.when(at < zs_count)
+            def _():
+                mean, level = merged(zz * 2 + c, at - 1)
+                zsend[at, 0:HD] = mean.astype(BF16)
+                high = level.astype(BF16).astype(F32)
+                middle = (level - high).astype(BF16).astype(F32)
+                low = level - high - middle
+                place = lax.broadcasted_iota(jnp.int32, (AUG - HD, rows), 0)
+                terms = jnp.where(place == 0, high, jnp.where(place == 1, middle, low))
+                zsend[at, HD:AUG] = terms.astype(BF16)
+                p_to_z(at).start()
 
         return carry
 
-    lax.fori_loop(1, zs_count + 1, pass_two, 0)
+    lax.fori_loop(1, zs_count + 2, pass_two, 0)
 
     means, levels = [], []
     mean, level = merged(z * 2 + c, zs_count - 1)
@@ -355,15 +419,16 @@
 
         @pl.when(d > 0)
         def _():
-            q_to_z(d).wait_send()
             p_to_z(d).wait_send()
 
         @pl.when(jnp.logical_and(z < zs_count - 1, d <= z))
         def _():
+            q_move(d, 1).wait_send()
             a_move(d, 1).wait_send()
 
         @pl.when(jnp.logical_and(z > 0, d >= z))
         def _():
+            q_move(d, -1).wait_send()
             a_move(d, -1).wait_send()
 
         @pl.when(d // per_head != my_head)
@@ -388,7 +453,7 @@
     out_rows = span // heads
     vmem = pl.BlockSpec(memory_space=pltpu.VMEM)
     smem = pl.BlockSpec(memory_space=pltpu.SMEM)
-    sems = [(zs,)] * 4 + [(3,)] * 2 + [(zs,)] * 4 + [(2, zs)] + [(zs,)] * 9
+    sems = [(2, zs)] + [(zs,)] * 3 + [(3,)] * 2 + [(zs,)] * 4 + [(2, zs)] + [(zs,)] * 9
     per_head = zs // heads
     return pl.pallas_call(
         functools.partial(kernel, zs, heads, toks, qph),
@@ -412,7 +477,10 @@
             pltpu.VMEM((per_head, 4 * toks, width), F32),
             pltpu.VMEM((zs, 4 * toks, width), BF16),
             pltpu.VMEM((zs, 4 * toks, width), BF16),
-        ] + [pltpu.SemaphoreType.DMA(count) for count in sems],
+        ]
+        + [pltpu.VMEM((cache + 2 * toks, rows // 2), F32)] * 4
+        + [pltpu.VMEM((cache + 2 * toks, rows // 2), BF16)] * 4
+        + [pltpu.SemaphoreType.DMA(count) for count in sems],
         compiler_params=pltpu.CompilerParams(
             collective_id=0, has_side_effects=True, vmem_limit_bytes=56 * 1024 * 1024
         ),

time: 77.8 us -> 72.4 us (0.931)
  Pallas kernels: 75.1 us -> 69.7 us
    pallas_call x1, Pallas kernels: 75.1 us -> 69.7 us  [body(): pl.pallas_call(functools.partial(kernel, zs, heads, toks, qph), out_shape...]
where the time goes in v1:
time: 72.4 us; the launch traced here: 72.2 us
  Pallas kernels  69.7 us (96%)
  local copies, waits for them, and re-layouts  1.87 us (3%)
    pallas_call x1, Pallas kernels, body(): pl.pallas_call(functools.partial(kernel, zs, heads, toks, qph), out_shape...  69.7 us
    unnamed x1, local copies, waits for them, and re-layouts  1.87 us

profile of v1, /device:TPU:0, one launch (start us, length us, event | category | flops | bytes accessed | tf_op | source)
XLA Modules:
  0.0 72.2 jit_solution(7697948347280320123)
XLA Ops:
  0.7 69.7 %shard_map.82 = bf16[512,512]{1,0:T(8,128)(2,1)} custom-call(bf16[64,1024]{1,0:T(8,128)(2,1)} %q_ref.1, bf16[1024,128]{1,0:T(8,128)(2,1)} %bitcast.3, bf16[1024,128]{1,0:T(8,128)(2,1)} %bitcast.4, bf16[64,128]{1,0:T(8,128)(2,1)} %nk_ref.1, bf16[64,128]{1,0:T(8,128)(2,1)} %nv_ref.1, s32[1]{0:T(128)S(6)} %copy.10.len_ref, s32[8,128]{1,0:T(8,128)} %bitcast.5, ...), custom_call_target="tpu_custom_call" | custom-call | tf_op jit(solution)/shard_map/pallas_call | solution.py:458
  70.3 1.9 %copy.11 = bf16[512,512]{1,0:T(8,128)(2,1)} copy(bf16[512,512]{1,0:T(8,128)(2,1)} %shard_map.82) | data formatting | bytes 1048576
